TPU v7x, 32 devices: a whole 2x2x4 slice. The times are simulated.
32 devices in a mesh: section: 2 (over core), group: 4 (over z), rep: 4 (over y, x).
Axes of the slice: x: 2, y: 2, z: 4, core: 2. Of those that a mesh axis runs over, the one named last changes fastest.
Arguments:
- latents: bfloat16 [32, 256, 384], P(('group', 'rep')), may hold values from -6 to 6
- cond: float32 [32, 384], P(('group', 'rep')), may hold values from -6 to 6
- cotangent: bfloat16 [32, 256, 384], P(('group', 'rep')), may hold values from -6 to 6
- live_count: int32 [16, 2], P(('group', 'rep')), may hold values from 0 to 1, as said below
- adaptive_weight: bfloat16 [2, 384, 2304], P('section', 'group'), may hold values from -0.3125 to 0.3125
- adaptive_bias: bfloat16 [2, 2304], P('section', 'group'), may hold values from 0.5 to 1.5
- query_key_value_weight: bfloat16 [2, 384, 1152], P('section', 'group'), may hold values from -0.15625 to 0.15625
- output_projection_weight: bfloat16 [2, 384, 384], P('section', 'group'), may hold values from -1.25 to 1.25
- first_dense_weight: bfloat16 [2, 384, 1536], P('section', 'group'), may hold values from -0.3125 to 0.3125
- first_dense_bias: bfloat16 [2, 1536], P('section', 'group'), may hold values from -3 to 3
- second_dense_weight: bfloat16 [2, 1536, 384], P('section', 'group'), may hold values from -0.15625 to 0.15625
Outputs:
- section_outputs: bfloat16 [2, 32, 256, 384], P('section', ('group', 'rep'))
- input_grads: float32 [2, 32, 256, 384], P('section', ('group', 'rep'))
- cond_grads: float32 [2, 32, 384], P('section', ('group', 'rep'))
- grad_ada: float32 [2, 384, 2304], P('section', 'group')
- grad_bada: float32 [2, 2304], P('section', 'group')
- grad_qkv: float32 [2, 384, 1152], P('section', 'group')
- grad_proj: float32 [2, 384, 384], P('section', 'group')
- grad_fc1: float32 [2, 384, 1536], P('section', 'group')
- grad_bfc1: float32 [2, 1536], P('section', 'group')
- grad_fc2: float32 [2, 1536, 384], P('section', 'group')
Inputs may be any that keep to these rules, and one draw needn't show every extreme that they name: live_count of a device block and micro-batch counts the real latents, which fill its first slots; the rest hold no latent. In every micro-batch one device block has 1 and another has none.
All inputs are finite; a program needn't handle non-finite values.
Results may differ from a plain program's by a relative error of at most 0.018.
Values may be sent and summed in bfloat16 or wider, within the bound.
A program may use at most 192 MiB of HBM per device.

v0:
```python
from functools import partial
import jax
import jax.numpy as jnp
from jax import lax
from jax.sharding import PartitionSpec as P

D = 384
HEADS = 6
HEAD_DIM = 64
FF = 1536
TOK = 256
MB = 2
SLOTS = 1
epsilon = 1e-06


def passed_along(value, axis, steps):
    count = lax.axis_size(axis)
    first, last = (max(0, -steps), min(count, count - steps))
    return lax.ppermute(value, axis, [(source, source + steps) for source in range(first, last)])


def for_sending(x):
    return jax.tree.map(lambda a: a.astype(jnp.bfloat16) if a.dtype == jnp.float32 else a, x)


def normalize(values):
    center = values - jnp.mean(values, axis=-1, keepdims=True)
    spread = jnp.mean(center * center, axis=-1, keepdims=True)
    return center * lax.rsqrt(spread + epsilon)


def modulate(values, scale_part, shift_part):
    return normalize(values) * (1.0 + scale_part[:, None, :]) + shift_part[:, None, :]


def heads_of(array, offset):
    count, length = (array.shape[0], array.shape[1])
    return array[..., offset * D : (offset + 1) * D].reshape(count, length, HEADS, HEAD_DIM)


def attention_scores(queries, keys_part):
    scores = jnp.einsum("snhe,smhe->shnm", queries, keys_part, preferred_element_type=jnp.float32)
    return scores * HEAD_DIM ** (-0.5)


def forward_block(input_rows, condition_vector, weights):
    (
        adaptive_weight,
        adaptive_bias,
        query_key_value_weight,
        output_projection_weight,
        first_dense_weight,
        first_dense_bias,
        second_dense_weight,
    ) = weights
    silu_low = jax.nn.silu(condition_vector).astype(jnp.bfloat16)
    modulation = jnp.dot(
        silu_low, adaptive_weight, preferred_element_type=jnp.float32
    ) + adaptive_bias.astype(jnp.float32)
    shift_attn, scale_attn, gate_attn, shift_mlp, scale_mlp, gate_mlp = jnp.split(
        modulation, 6, axis=-1
    )
    widened = input_rows.astype(jnp.float32)
    normed_reduced = modulate(widened, scale_attn, shift_attn).astype(jnp.bfloat16)
    triple_low = jnp.dot(
        normed_reduced, query_key_value_weight, preferred_element_type=jnp.float32
    ).astype(jnp.bfloat16)
    queries = heads_of(triple_low, 0)
    keys_part = heads_of(triple_low, 1)
    values_part = heads_of(triple_low, 2)
    scores = attention_scores(queries, keys_part)
    highest = jnp.max(scores, axis=-1, keepdims=True)
    log_total = highest + jnp.log(jnp.sum(jnp.exp(scores - highest), axis=-1, keepdims=True))
    probs_low = jnp.exp(scores - log_total).astype(jnp.bfloat16)
    mixed = jnp.einsum(
        "shnm,smhe->snhe", probs_low, values_part, preferred_element_type=jnp.float32
    )
    mixed_reduced = mixed.reshape(input_rows.shape).astype(jnp.bfloat16)
    attended = jnp.dot(mixed_reduced, output_projection_weight, preferred_element_type=jnp.float32)
    middle = widened + gate_attn[:, None, :] * attended
    second_low = modulate(middle, scale_mlp, shift_mlp).astype(jnp.bfloat16)
    hidden = jnp.dot(
        second_low, first_dense_weight, preferred_element_type=jnp.float32
    ) + first_dense_bias.astype(jnp.float32)
    active_low = jax.nn.gelu(hidden, approximate=True).astype(jnp.bfloat16)
    branch = jnp.dot(active_low, second_dense_weight, preferred_element_type=jnp.float32)
    result = middle + gate_mlp[:, None, :] * branch
    kept_state = (
        input_rows,
        condition_vector,
        modulation,
        normed_reduced,
        triple_low,
        log_total[..., 0],
        mixed_reduced,
        attended,
        middle,
        second_low,
        hidden,
        active_low,
        branch,
    )
    return (result, kept_state)


def forward_empty(input_rows, condition_vector, weights):
    count, length = (input_rows.shape[0], input_rows.shape[1])
    rows_float = jnp.zeros((count, length, D), jnp.float32)
    rows_low = jnp.zeros((count, length, D), jnp.bfloat16)
    kept_state = (
        rows_low,
        jnp.zeros((count, D), jnp.float32),
        jnp.zeros((count, 6 * D), jnp.float32),
        rows_low,
        jnp.zeros((count, length, 3 * D), jnp.bfloat16),
        jnp.zeros((count, HEADS, length), jnp.float32),
        rows_low,
        rows_float,
        rows_float,
        rows_low,
        jnp.zeros((count, length, FF), jnp.float32),
        jnp.zeros((count, length, FF), jnp.bfloat16),
        rows_float,
    )
    return (rows_float, kept_state)


def backward_block(out_grad, kept_state, weights):
    (
        adaptive_weight,
        adaptive_bias,
        query_key_value_weight,
        output_projection_weight,
        first_dense_weight,
        first_dense_bias,
        second_dense_weight,
    ) = weights
    (
        input_rows,
        condition_vector,
        modulation,
        normed_reduced,
        triple_low,
        log_total,
        mixed_reduced,
        attended,
        middle,
        second_low,
        hidden,
        active_low,
        branch,
    ) = kept_state
    count, length = (input_rows.shape[0], input_rows.shape[1])
    shift_attn, scale_attn, gate_attn, shift_mlp, scale_mlp, gate_mlp = jnp.split(
        modulation, 6, axis=-1
    )
    grad_gate_mlp = jnp.sum(out_grad * branch, axis=1)
    branch_low = (gate_mlp[:, None, :] * out_grad).astype(jnp.bfloat16)
    grad_fc2 = jnp.einsum("snf,snd->fd", active_low, branch_low, preferred_element_type=jnp.float32)
    grad_active = jnp.einsum(
        "snd,fd->snf", branch_low, second_dense_weight, preferred_element_type=jnp.float32
    )
    unused, gelu_back = jax.vjp(partial(jax.nn.gelu, approximate=True), hidden)
    hidden_low = gelu_back(grad_active)[0].astype(jnp.bfloat16)
    grad_bias = jnp.sum(hidden_low, axis=(0, 1), dtype=jnp.float32)
    grad_fc1 = jnp.einsum("snd,snf->df", second_low, hidden_low, preferred_element_type=jnp.float32)
    grad_second = jnp.einsum(
        "snf,df->snd", hidden_low, first_dense_weight, preferred_element_type=jnp.float32
    )
    unused, norm_back = jax.vjp(modulate, middle, scale_mlp, shift_mlp)
    grad_middle, grad_scale_mlp, grad_shift_mlp = norm_back(grad_second)
    grad_middle = grad_middle + out_grad
    grad_gate_attn = jnp.sum(grad_middle * attended, axis=1)
    attended_reduced = (gate_attn[:, None, :] * grad_middle).astype(jnp.bfloat16)
    grad_proj = jnp.einsum(
        "row,rol->wl", mixed_reduced, attended_reduced, preferred_element_type=jnp.float32
    )
    mixed_grad_low = jnp.einsum(
        "lqa,ia->lqi",
        attended_reduced,
        output_projection_weight,
        preferred_element_type=jnp.float32,
    ).astype(jnp.bfloat16)
    heads_grad = mixed_grad_low.reshape(count, length, HEADS, HEAD_DIM)
    queries = heads_of(triple_low, 0)
    keys_part = heads_of(triple_low, 1)
    values_part = heads_of(triple_low, 2)
    probs = jnp.exp(attention_scores(queries, keys_part) - log_total[..., None])
    probs_low = probs.astype(jnp.bfloat16)
    grad_values = jnp.einsum(
        "shnm,snhe->smhe", probs_low, heads_grad, preferred_element_type=jnp.float32
    )
    grad_probs = jnp.einsum(
        "snhe,smhe->shnm", heads_grad, values_part, preferred_element_type=jnp.float32
    )
    scores_low = (
        probs * (grad_probs - jnp.sum(grad_probs * probs, axis=-1, keepdims=True))
    ).astype(jnp.bfloat16)
    grad_queries = jnp.einsum(
        "shnm,smhe->snhe", scores_low, keys_part, preferred_element_type=jnp.float32
    ) * HEAD_DIM ** (-0.5)
    grad_keys = jnp.einsum(
        "shnm,snhe->smhe", scores_low, queries, preferred_element_type=jnp.float32
    ) * HEAD_DIM ** (-0.5)
    triple_gradient_reduced = jnp.concatenate(
        [
            grad_queries.reshape(count, length, D),
            grad_keys.reshape(count, length, D),
            grad_values.reshape(count, length, D),
        ],
        axis=-1,
    ).astype(jnp.bfloat16)
    grad_qkv = jnp.einsum(
        "row,rol->wl", normed_reduced, triple_gradient_reduced, preferred_element_type=jnp.float32
    )
    grad_normed = jnp.einsum(
        "lqa,ia->lqi",
        triple_gradient_reduced,
        query_key_value_weight,
        preferred_element_type=jnp.float32,
    )
    unused, first_back = jax.vjp(modulate, input_rows.astype(jnp.float32), scale_attn, shift_attn)
    grad_inputs, grad_scale_attn, grad_shift_attn = first_back(grad_normed)
    grad_inputs = grad_inputs + grad_middle
    modulation_low = jnp.concatenate(
        [
            grad_shift_attn,
            grad_scale_attn,
            grad_gate_attn,
            grad_shift_mlp,
            grad_scale_mlp,
            grad_gate_mlp,
        ],
        axis=-1,
    ).astype(jnp.bfloat16)
    grad_bada = jnp.sum(modulation_low, axis=0, dtype=jnp.float32)
    silu_low = jax.nn.silu(condition_vector).astype(jnp.bfloat16)
    grad_ada = jnp.dot(silu_low.T, modulation_low, preferred_element_type=jnp.float32)
    grad_silu = jnp.dot(modulation_low, adaptive_weight.T, preferred_element_type=jnp.float32)
    unused, silu_back = jax.vjp(jax.nn.silu, condition_vector)
    grad_condition = silu_back(grad_silu)[0]
    return (
        grad_inputs,
        grad_condition,
        (grad_ada, grad_bada, grad_qkv, grad_proj, grad_fc1, grad_bias, grad_fc2),
    )


def backward_empty(out_grad, kept_state, weights):
    count = out_grad.shape[0]
    grads = tuple((jnp.zeros(array.shape, jnp.float32) for array in weights))
    return (jnp.zeros(out_grad.shape, jnp.float32), jnp.zeros((count, D), jnp.float32), grads)


def stripped(gathered):
    return tuple((array[0] for array in gathered))


def body(
    latents,
    cond,
    cotangent,
    live_count,
    adaptive_weight,
    adaptive_bias,
    query_key_value_weight,
    output_projection_weight,
    first_dense_weight,
    first_dense_bias,
    second_dense_weight,
):
    is_first = lax.axis_index("section") == 0
    inputs_all = latents.reshape(MB, SLOTS, TOK, D)
    conds_all = cond.reshape(MB, SLOTS, D)
    tangents_all = cotangent.reshape(MB, SLOTS, TOK, D)
    live = (jnp.arange(SLOTS, dtype=jnp.int32)[None, :] < live_count[0][:, None]).astype(
        jnp.float32
    )
    kept_weights = stripped(
        (
            lax.all_gather(adaptive_weight, "group", axis=1, tiled=True),
            lax.all_gather(adaptive_bias, "group", axis=1, tiled=True),
            lax.all_gather(query_key_value_weight, "group", axis=1, tiled=True),
            lax.all_gather(output_projection_weight, "group", axis=1, tiled=True),
            lax.all_gather(first_dense_weight, "group", axis=1, tiled=True),
            lax.all_gather(first_dense_bias, "group", axis=1, tiled=True),
            lax.all_gather(second_dense_weight, "group", axis=1, tiled=True),
        )
    )
    received = jnp.zeros((SLOTS, TOK, D), jnp.bfloat16)
    forward_out = []
    states = []
    for moment in range(MB + 1):
        weights = kept_weights
        own_rows = inputs_all[min(moment, MB - 1)]
        rows_in = jnp.where(is_first, own_rows, received)
        cond_in = jnp.where(is_first, conds_all[min(moment, MB - 1)], conds_all[max(moment - 1, 0)])
        active = jnp.where(is_first, moment < MB, moment >= 1)
        result, kept_state = lax.cond(
            active, forward_block, forward_empty, rows_in, cond_in, weights
        )
        result_low = result.astype(jnp.bfloat16)
        forward_out.append(result_low)
        states.append(kept_state)
        if moment < MB:
            received = passed_along(result_low, "section", 1)
    grad_recv = jnp.zeros((SLOTS, TOK, D), jnp.bfloat16)
    cond_recv = jnp.zeros((SLOTS, D), jnp.bfloat16)
    backward_out = []
    owned = None
    totals = None
    for moment in range(MB + 1):
        weights = kept_weights
        earlier = max(MB - 1 - moment, 0)
        out_grad = jnp.where(
            is_first,
            grad_recv.astype(jnp.float32),
            tangents_all[earlier].astype(jnp.float32) * live[earlier][:, None, None],
        )
        kept_state = states[MB - moment]
        active = jnp.where(is_first, moment >= 1, moment < MB)
        grad_rows, grad_cond, grads = lax.cond(
            active, backward_block, backward_empty, out_grad, kept_state, weights
        )
        rows_low = grad_rows.astype(jnp.bfloat16)
        cond_low = grad_cond.astype(jnp.bfloat16)
        backward_out.append((grad_rows, grad_cond, rows_low, cond_low, cond_recv))
        totals = (
            grads
            if totals is None
            else jax.tree.map(lambda former, latter: former + latter, totals, grads)
        )
        if moment < MB:
            grad_recv, cond_recv = passed_along((rows_low, cond_low), "section", -1)
    owned = jax.tree.map(
        lambda part: part.astype(jnp.float32),
        lax.psum_scatter(for_sending(totals), "group", scatter_dimension=0, tiled=True),
    )
    owned = jax.tree.map(lambda part: part.astype(jnp.float32), lax.psum(for_sending(owned), "rep"))
    outputs_list = []
    input_list = []
    cond_list = []
    for batch in range(MB):
        alive = live[batch].astype(jnp.bfloat16)[:, None, None]
        outputs_list.append(jnp.where(is_first, forward_out[batch], forward_out[batch + 1]) * alive)
        early = backward_out[MB - batch]
        late = backward_out[MB - 1 - batch]
        input_list.append(jnp.where(is_first, early[0], late[2].astype(jnp.float32)))
        cond_list.append(
            jnp.where(
                is_first, early[1] + early[4].astype(jnp.float32), late[3].astype(jnp.float32)
            )
        )
    section_outputs = jnp.concatenate(outputs_list, axis=0)[None]
    input_grads = jnp.concatenate(input_list, axis=0)[None]
    cond_grads = jnp.concatenate(cond_list, axis=0)[None]
    return (
        section_outputs,
        input_grads,
        cond_grads,
        owned[0][None],
        owned[1][None],
        owned[2][None],
        owned[3][None],
        owned[4][None],
        owned[5][None],
        owned[6][None],
    )


def solution(mesh):
    return jax.shard_map(
        body,
        mesh=mesh,
        in_specs=(
            P(("group", "rep"), None, None),
            P(("group", "rep"), None),
            P(("group", "rep"), None, None),
            P(("group", "rep"), None),
            P("section", "group", None),
            P("section", "group"),
            P("section", "group", None),
            P("section", "group", None),
            P("section", "group", None),
            P("section", "group"),
            P("section", "group", None),
        ),
        out_specs=(
            P("section", ("group", "rep"), None, None),
            P("section", ("group", "rep"), None, None),
            P("section", ("group", "rep"), None),
            P("section", "group", None),
            P("section", "group"),
            P("section", "group", None),
            P("section", "group", None),
            P("section", "group", None),
            P("section", "group"),
            P("section", "group", None),
        ),
        check_vma=False,
    )
```

profile of v0, /device:TPU:0, one launch (start us, length us, event | category | flops | bytes accessed | tf_op | source)
XLA Modules:
  0.0 573.9 jit_solution(1712281635695127555)
XLA Ops:
  12.1 13.8 %all_gather.26 = bf16[1,1536]{1,0:T(2,128)(2,1)S(1)} all-gather(bf16[1,384]{1,0:T(2,128)(2,1)} %param.28), channel_id=1, replica_groups=mesh['section'=2,'group'=4,'rep'=4] {'group'}, dimensions={1}, use_global_device_ids=true | all-gather | bytes 3840 | tf_op jit(solution)/shard_map/all_gather | solution.py:287
  30.5 11.2 %all-reduce = bf16[2304]{0:T(1024)(128)(2,1)S(1)} all-reduce(bf16[2304]{0:T(1024)(128)(2,1)S(1)} %dynamic-update-slice), channel_id=1, replica_groups=mesh['section'=2,'group'=4,'rep'=4] {'group'}, use_global_device_ids=true, to_apply=%add | all-reduce | flops 2304 | bytes 9216 | tf_op jit(solution)/shard_map/squeeze | solution.py:257
  41.6 14.0 %all_gather.24 = bf16[1,384,384]{2,1,0:T(8,128)(2,1)S(1)} all-gather(bf16[1,96,384]{2,1,0:T(8,128)(2,1)S(1)} %copy-done.114), channel_id=1, replica_groups=mesh['section'=2,'group'=4,'rep'=4] {'group'}, dimensions={1}, use_global_device_ids=true | all-gather | bytes 368640 | tf_op jit(solution)/shard_map/all_gather | solution.py:285
  57.5 31.4 %all_gather.23 = bf16[1,384,1152]{2,1,0:T(8,128)(2,1)S(1)} all-gather(bf16[1,96,1152]{2,1,0:T(8,128)(2,1)S(1)} %copy-done.102), channel_id=1, replica_groups=mesh['section'=2,'group'=4,'rep'=4] {'group'}, dimensions={1}, use_global_device_ids=true | all-gather | bytes 1105920 | tf_op jit(solution)/shard_map/all_gather | solution.py:284
  88.9 41.7 %all-gather.4.cloned.1.call-done = bf16[1,384,2304]{2,1,0:T(8,128)(2,1)} async-done(((bf16[1,96,2304]{2,1,0:T(8,128)(2,1)}), bf16[1,384,2304]{2,1,0:T(8,128)(2,1)}) %all-gather.4.cloned.1.call-update) | async-done | bytes 1769488 | tf_op jit(solution)/shard_map/all_gather | solution.py:282
  130.6 13.2 %conditional.4 = (bf16[1,256,384]{2,1,0:T(8,128)(2,1)S(1)}, f32[1,384]{1,0:T(1,128)}, f32[1,2304]{1,0:T(1,128)S(1)}, bf16[1,256,384]{2,1,0:T(8,128)(2,1)}, bf16[...) conditional(s32[]{:T(128)} %convert_element_type.491, () %tuple.65, ...), branch_computations={%region_0.1_spmd, %region_1.8_spmd} | conditional | flops 1021386368 | bytes 41346496 | solution.py:300
  130.6 1.8 convolution_reduce_fusion
  137.2 1.7 convolution_add_fusion
  138.9 2.8 fusion.16
  141.8 1.9 fusion.29
  145.8 1.8 convolution_reduce_fusion.2
  157.7 10.2 %conditional.5 = (bf16[1,256,384]{2,1,0:T(8,128)(2,1)S(1)}, f32[1,384]{1,0:T(1,128)}, f32[1,2304]{1,0:T(1,128)}, bf16[1,256,384]{2,1,0:T(8,128)(2,1)}, bf16[1,25...) conditional(s32[]{:T(128)} %convert_element_type.509, () %tuple.67, ...), branch_computations={%region_14.15_spmd, %region_15.22_spmd} | conditional | flops 1021386368 | bytes 41874824 | solution.py:300
  167.9 9.5 %conditional.6 = (f32[384,2304]{1,0:T(8,128)}, f32[2304]{0:T(1024)S(1)}, f32[1536]{0:T(1024)S(1)}, bf16[1,256,384]{2,1,0:T(8,128)(2,1)S(1)}, bf16[1,384]{1,0:T(2...) conditional(s32[]{:T(128)} %convert_element_type.509, () %tuple.70, ...), branch_computations={%region_22.23_spmd, %region_23.40_spmd} | conditional | flops 2089162752 | bytes 87958680 | solution.py:323
  173.6 1.7 broadcast.903.clone
  175.4 2.0 broadcast.899
  178.9 92.8 %collective-permute-done.2 = bf16[1,256,384]{2,1,0:T(8,128)(2,1)S(1)} collective-permute-done((bf16[1,256,384]{2,1,0:T(8,128)(2,1)S(1)}, bf16[1,256,384]{2,1,0:T(8,128)(2,1)S(1)}, u32[]{:S(2)}, u32[]{:S(2)}) %collective-permute-start.2) | collective-permute-done | bytes 196640 | tf_op jit(solution)/shard_map/ppermute | solution.py:20
  271.8 4.6 convert_reduce_fusion.8
  278.4 2.1 fusion.169
  282.3 1.8 copy.127
  291.7 2.0 collective-permute-done.3
  294.6 58.3 %conditional.7 = (f32[1,256,384]{2,1,0:T(8,128)}, f32[1,384]{1,0:T(1,128)}, f32[384,2304]{1,0:T(8,128)}, f32[2304]{0:T(1024)}, f32[1536]{0:T(1024)}, /*index=5*/...) conditional(s32[]{:T(128)} %convert_element_type.491, () %tuple.69, ...), branch_computations={%region_45.46_spmd, %region_46.63_spmd} | conditional | flops 2088473856 | bytes 92844544 | solution.py:323
  298.3 2.0 convert_reduce_fusion.7
  300.2 1.8 multiply_reduce_fusion.7
  302.1 3.6 convert_reduce_fusion.5
  311.3 1.9 multiply_reduce_fusion.8
  317.3 2.1 convolution_bitcast_fusion.9
  319.4 2.1 copy.164
  321.5 2.1 copy.131
  332.1 2.0 add_add_fusion.5
  336.5 1.9 copy.162
  338.4 3.3 convolution_bitcast_fusion.5
  341.7 3.2 copy.168
  344.9 2.0 convolution_bitcast_fusion.6
  346.9 3.2 copy.166
  350.1 2.9 broadcast_multiply_fusion.7
  352.9 2.3 add_convert_fusion.7
  355.4 3.7 add_convert_fusion.6
  359.5 4.1 add_convert_fusion.5
  363.7 5.7 add_convert_fusion.4
  371.8 4.9 add_convert_fusion.3
  381.1 18.7 %reduce-scatter.8.cloned.1.call-done = bf16[96,1152]{1,0:T(8,128)(2,1)} async-done(((bf16[384,1152]{1,0:T(8,128)(2,1)}), bf16[96,1152]{1,0:T(8,128)(2,1)}) %reduce-scatter.8.cloned.1.call-update) | async-done | bytes 221200 | tf_op jit(solution)/shard_map/reduce_scatter | solution.py:338
  399.8 30.4 %reduce-scatter.12.cloned.1.call-done = bf16[96,1536]{1,0:T(8,128)(2,1)} async-done(((bf16[384,1536]{1,0:T(8,128)(2,1)}), bf16[96,1536]{1,0:T(8,128)(2,1)}) %reduce-scatter.12.cloned.1.call-update) | async-done | bytes 294928 | tf_op jit(solution)/shard_map/reduce_scatter | solution.py:338
  430.2 30.2 %reduce-scatter.14.cloned.1.call-done = bf16[384,384]{1,0:T(8,128)(2,1)} async-done(((bf16[1536,384]{1,0:T(8,128)(2,1)}), bf16[384,384]{1,0:T(8,128)(2,1)}) %reduce-scatter.14.cloned.1.call-update) | async-done | bytes 294928 | tf_op jit(solution)/shard_map/reduce_scatter | solution.py:338
  460.4 39.5 %reduce-scatter.6.cloned.1.call-done = bf16[96,2304]{1,0:T(8,128)(2,1)} async-done(((bf16[384,2304]{1,0:T(8,128)(2,1)}), bf16[96,2304]{1,0:T(8,128)(2,1)}) %reduce-scatter.6.cloned.1.call-update) | async-done | bytes 442384 | tf_op jit(solution)/shard_map/reduce_scatter | solution.py:338
  503.3 17.0 %all-reduce.5 = (bf16[2304]{0:T(1024)(128)(2,1)S(1)}, bf16[1536]{0:T(1024)(128)(2,1)S(1)}) all-reduce(bf16[2304]{0:T(1024)(128)(2,1)S(1)} %add_convert_fusion.9, bf16[1536]{0:T(1024)(128)(2,1)S(1)} %add_convert_fusion.10), channel_id=3, replica_groups=mesh['section'=2,'group'=4,'rep'=4] {'group'}, use_global_device_ids=true, to_apply=%region_71.72.clone | all-reduce | flops 3840 | bytes 15360
  520.4 9.8 %all-reduce.3 = (bf16[1,576]{1,0:T(2,128)(2,1)S(1)}, bf16[1,384]{1,0:T(2,128)(2,1)S(1)}) all-reduce(bf16[1,576]{1,0:T(2,128)(2,1)S(1)} %broadcast_in_dim.142, bf16[1,384]{1,0:T(2,128)(2,1)S(1)} %broadcast_in_dim.172), channel_id=1, replica_groups=mesh['section'=2,'group'=4,'rep'=4] {'rep'}, use_global_device_ids=true, to_apply=%region_72.73 | all-reduce | flops 960 | bytes 3840 | tf_op jit(solution)/shard_map/psum | solution.py:340
  534.7 26.4 %all-reduce.8.cloned.1.call-done = (bf16[1,96,2304]{2,1,0:T(8,128)(2,1)}, bf16[1,96,1152]{2,1,0:T(8,128)(2,1)}, bf16[1,96,384]{2,1,0:T(8,128)(2,1)}, bf16[1,96,1536]{2,1,0:T(8,128)(2,1)}, bf16[1,384,384]{2,1,0:T(8,128)(2,1)}) async-done(((bf16[1,96,2304]{2,1,0:T(8,128)(2,1)}, bf16[1,96,1152]{2,1,0:T(8,128)(2,1)}, bf16[1,96,384]{2,1,0:T(8,128)(2,1)}, bf16[1,96,1536]{2,1,0:T(8,128)(2,1)}, ...) | async-done | bytes 1327120 | tf_op jit(solution)/shard_map/psum | solution.py:340
  562.7 2.0 broadcast_in_dim.141
  (501 shorter events, 96.0 us)
Async XLA Ops:
  7.2 123.4 %copy-start.64 = (bf16[2,256,384]{2,1,0:T(8,128)(2,1)S(1)}, bf16[2,256,384]{2,1,0:T(8,128)(2,1)}, u32[]{:S(2)}) copy-start(bf16[2,256,384]{2,1,0:T(8,128)(2,1)} %param.19) | copy-start | bytes 1179652
  7.2 34.4 %copy-start.114 = (bf16[1,96,384]{2,1,0:T(8,128)(2,1)S(1)}, bf16[1,96,384]{2,1,0:T(8,128)(2,1)}, u32[]{:S(2)}) copy-start(bf16[1,96,384]{2,1,0:T(8,128)(2,1)} %param.26) | copy-start | bytes 221188
  7.2 48.5 %copy-start.150 = (f32[2,384]{1,0:T(2,128)S(1)}, f32[2,384]{1,0:T(2,128)}, u32[]{:S(2)}) copy-start(f32[2,384]{1,0:T(2,128)} %param.20) | copy-start | bytes 9220
  7.2 50.3 %copy-start.102 = (bf16[1,96,1152]{2,1,0:T(8,128)(2,1)S(1)}, bf16[1,96,1152]{2,1,0:T(8,128)(2,1)}, u32[]{:S(2)}) copy-start(bf16[1,96,1152]{2,1,0:T(8,128)(2,1)} %param.25) | copy-start | bytes 663556
  7.2 81.6 %all-gather.6.cloned.1.call-start = ((), (), s32[]{:S(2)}) async-start(), calls=%async_computation.6 | async-start | bytes 1474560 | tf_op jit(solution)/shard_map/all_gather | solution.py:286
  8.0 80.9 %all-gather.8.cloned.1.call-start = ((), (), s32[]{:S(2)}) async-start(), calls=%async_computation.7 | async-start | bytes 1474560 | tf_op jit(solution)/shard_map/all_gather | solution.py:288
  8.7 121.8 %all-gather.4.cloned.1.call-start = ((), (), s32[]{:S(2)}) async-start(), calls=%async_computation.5 | async-start | bytes 2211840 | tf_op jit(solution)/shard_map/all_gather | solution.py:282
  9.4 371.7 %reduce-scatter.10.cloned.1.call-start = ((), (), s32[]{:S(2)}) async-start(), calls=%async_computation.10 | async-start | bytes 368640 | tf_op jit(solution)/shard_map/reduce_scatter | solution.py:338
  25.9 104.6 %copy-start.115 = (bf16[1536]{0:T(1024)(128)(2,1)}, bf16[1536]{0:T(1024)(128)(2,1)S(1)}, u32[]{:S(2)}) copy-start(bf16[1536]{0:T(1024)(128)(2,1)S(1)} %reduce.132) | copy-start | bytes 9220
  55.7 95.3 %copy-start.1 = (bf16[1,384,384]{2,1,0:T(8,128)(2,1)}, bf16[1,384,384]{2,1,0:T(8,128)(2,1)S(1)}, u32[]{:S(2)}) copy-start(bf16[1,384,384]{2,1,0:T(8,128)(2,1)S(1)} %all_gather.24) | copy-start | bytes 884740
  88.9 59.8 %copy-start.6 = (bf16[1,384,1152]{2,1,0:T(8,128)(2,1)}, bf16[1,384,1152]{2,1,0:T(8,128)(2,1)S(1)}, u32[]{:S(2)}) copy-start(bf16[1,384,1152]{2,1,0:T(8,128)(2,1)S(1)} %all_gather.23) | copy-start | bytes 2654212
  144.3 4.9 copy-start.25
  144.3 4.9 copy-start.36
  144.3 4.9 copy-start.103
  144.3 3.9 collective-permute-start
  155.3 2.3 collective-permute-start.1
  177.4 94.3 %copy-start.110 = (f32[2304]{0:T(1024)}, f32[2304]{0:T(1024)S(1)}, u32[]{:S(2)}) copy-start(f32[2304]{0:T(1024)S(1)} %get-tuple-element.381) | copy-start | bytes 27652
  177.4 94.3 %copy-start.127 = (f32[1536]{0:T(1024)}, f32[1536]{0:T(1024)S(1)}, u32[]{:S(2)}) copy-start(f32[1536]{0:T(1024)S(1)} %get-tuple-element.389) | copy-start | bytes 18436
  177.4 94.3 %collective-permute-start.2 = (bf16[1,256,384]{2,1,0:T(8,128)(2,1)S(1)}, bf16[1,256,384]{2,1,0:T(8,128)(2,1)S(1)}, u32[]{:S(2)}, u32[]{:S(2)}) collective-permute-start(bf16[1,256,384]{2,1,0:T(8,128)(2,1)S(1)} %get-tuple-element.363), channel_id=1, source_target_pairs={{16,0},{17,1},{18,2},{19,3},{20,4},{21,5},{22,6},{23,7},{24,8},{25... | collective-permute-start | bytes 589832 | tf_op jit(solution)/shard_map/ppermute | solution.py:20
  271.7 6.7 %copy-start.91 = (bf16[1,256,384]{2,1,0:T(8,128)(2,1)}, bf16[1,256,384]{2,1,0:T(8,128)(2,1)S(1)}, u32[]{:S(2)}) copy-start(bf16[1,256,384]{2,1,0:T(8,128)(2,1)S(1)} %collective-permute-done.2) | copy-start | bytes 589828
  271.7 4.7 copy-start.15
  271.7 4.7 copy-start.21
  289.2 5.4 copy-start.60
  289.2 5.4 copy-start.3
  289.2 5.4 copy-start.11
  289.2 5.3 copy-start.26
  289.2 5.3 copy-start.113
  290.4 3.3 collective-permute-start.3
  300.2 5.4 copy-start.166
  327.1 4.8 copy-start.178
  328.4 5.8 %copy-start.137 = (f32[1,384]{1,0:T(1,128)S(1)}, f32[1,384]{1,0:T(1,128)}, u32[]{:S(2)}) copy-start(f32[1,384]{1,0:T(1,128)} %get-tuple-element.282) | copy-start | bytes 4612 | tf_op jit(solution)/shard_map/cond
  328.4 5.8 %copy-start.172 = (f32[1,384]{1,0:T(1,128)S(1)}, f32[1,384]{1,0:T(1,128)}, u32[]{:S(2)}) copy-start(f32[1,384]{1,0:T(1,128)} %get-tuple-element.680) | copy-start | bytes 4612 | tf_op jit(solution)/shard_map/cond
  355.3 44.5 %reduce-scatter.8.cloned.1.call-start = ((), (), s32[]{:S(2)}) async-start(), calls=%async_computation.9 | async-start | bytes 1105920 | tf_op jit(solution)/shard_map/reduce_scatter | solution.py:338
  359.2 71.0 %reduce-scatter.12.cloned.1.call-start = ((), (), s32[]{:S(2)}) async-start(), calls=%async_computation.11 | async-start | bytes 1474560 | tf_op jit(solution)/shard_map/reduce_scatter | solution.py:338
  363.6 96.8 %reduce-scatter.14.cloned.1.call-start = ((), (), s32[]{:S(2)}) async-start(), calls=%async_computation.12 | async-start | bytes 1474560 | tf_op jit(solution)/shard_map/reduce_scatter | solution.py:338
  363.7 5.8 %copy-start.181 = (bf16[384]{0:T(512)(128)(2,1)S(1)}, bf16[384]{0:T(512)(128)(2,1)}, u32[]{:S(2)}) copy-start(bf16[384]{0:T(512)(128)(2,1)} %get-tuple-element.687) | copy-start | bytes 2308
  363.7 5.8 %copy-start.59 = (f32[256,384]{1,0:T(8,128)S(1)}, f32[256,384]{1,0:T(8,128)}, u32[]{:S(2)}) copy-start(f32[256,384]{1,0:T(8,128)} %copy-done.58) | copy-start | bytes 1179652
  369.4 130.5 %reduce-scatter.6.cloned.1.call-start = ((), (), s32[]{:S(2)}) async-start(), calls=%async_computation.8 | async-start | bytes 2211840 | tf_op jit(solution)/shard_map/reduce_scatter | solution.py:338
  376.7 123.2 %copy-start.149 = (f32[1,384]{1,0:T(1,128)S(1)}, f32[1,384]{1,0:T(1,128)}, u32[]{:S(2)}) copy-start(f32[1,384]{1,0:T(1,128)} %get-tuple-element.688) | copy-start | bytes 4612
  376.7 184.3 %all-reduce.8.cloned.1.call-start = ((), (), s32[]{:S(2)}) async-start(), calls=%async_computation.13 | async-start | bytes 2654208 | tf_op jit(solution)/shard_map/psum | solution.py:340
  378.9 152.5 %collective-permute-start.5 = (bf16[1,384]{1,0:T(2,128)(2,1)S(1)}, bf16[1,384]{1,0:T(2,128)(2,1)S(1)}, u32[]{:S(2)}, u32[]{:S(2)}) collective-permute-start(bf16[1,384]{1,0:T(2,128)(2,1)S(1)} %copy-done.183), channel_id=1, source_target_pairs={{16,0},{17,1},{18,2},{19,3},{20,4},{21,5},{22,6},{23,7},{24,8},{25... | collective-permute-start | bytes 2312 | tf_op jit(solution)/shard_map/ppermute | solution.py:20
  381.1 120.8 %copy-start.128 = (f32[1536]{0:T(1024)S(1)}, f32[1536]{0:T(1024)}, u32[]{:S(2)}) copy-start(f32[1536]{0:T(1024)} %copy-done.127) | copy-start | bytes 18436
  381.1 120.8 %copy-start.171 = (f32[1536]{0:T(1024)S(1)}, f32[1536]{0:T(1024)}, u32[]{:S(2)}) copy-start(f32[1536]{0:T(1024)} %get-tuple-element.772) | copy-start | bytes 18436
  499.9 31.5 %copy-start.173 = (f32[1,384]{1,0:T(1,128)S(1)}, f32[1,384]{1,0:T(1,128)}, u32[]{:S(2)}) copy-start(f32[1,384]{1,0:T(1,128)} %get-tuple-element.378) | copy-start | bytes 4612
  499.9 32.8 %copy-start.76 = (bf16[1,256,384]{2,1,0:T(8,128)(2,1)S(1)}, bf16[1,256,384]{2,1,0:T(8,128)(2,1)}, u32[]{:S(2)}) copy-start(bf16[1,256,384]{2,1,0:T(8,128)(2,1)} %copy-done.75) | copy-start | bytes 589828
  499.9 33.8 %copy-start.55 = (f32[1,256,384]{2,1,0:T(8,128)S(1)}, f32[1,256,384]{2,1,0:T(8,128)}, u32[]{:S(2)}) copy-start(f32[1,256,384]{2,1,0:T(8,128)} %get-tuple-element.748) | copy-start | bytes 1179652
  500.5 30.9 %collective-permute-start.4 = (bf16[1,384]{1,0:T(2,128)(2,1)S(1)}, bf16[1,384]{1,0:T(2,128)(2,1)S(1)}, u32[]{:S(2)}, u32[]{:S(2)}) collective-permute-start(bf16[1,384]{1,0:T(2,128)(2,1)S(1)} %get-tuple-element.770), channel_id=1, source_target_pairs={{16,0},{17,1},{18,2},{19,3},{20,4},{21,5},{22,6},{23,7},{24,8},{25... | collective-permute-start | bytes 2312 | tf_op jit(solution)/shard_map/ppermute | solution.py:20
  561.0 5.3 copy-start.99
  (121 other events, 286.0 us)
Sparse Core Ops, SparseCore 0:
  9.6 34.4 all-gather.5
  45.7 42.9 all-gather.7
  90.3 40.1 all-gather.3
  355.4 18.7 reduce-scatter.9
  376.9 22.8 reduce-scatter.7
  402.0 28.1 reduce-scatter.11
  432.5 27.8 reduce-scatter.13
  462.8 37.0 reduce-scatter.5
  504.0 57.0 all-reduce.7
where the time goes:
time: 584 us; the launch traced here: 574 us
  waiting for transfers between devices  284 us (49%)
  blocking collectives  97.2 us (17%)
  matrix products  60.4 us (10%)
  local copies, waits for them, and re-layouts  52.3 us (9%)
  other arithmetic  51.3 us (9%)
  between operations  18.8 us (3%)
  starting transfers between devices  8.63 us (1%)
    reduce_scatter x5, waiting for transfers between devices, body(): lax.psum_scatter(for_sending(totals), 'group', scatter_dimension=0, tiled...  119 us
    ppermute x6, waiting for transfers between devices, passed_along(): lax.ppermute(value, axis, [(source, source + steps) for source in range(f...  95.1 us
    all_gather x1, waiting for transfers between devices, body(): lax.all_gather(adaptive_weight, 'group', axis=1, tiled=True)  41.7 us
    all_gather x1, blocking collectives, body(): lax.all_gather(query_key_value_weight, 'group', axis=1, tiled=True)  31.4 us
    psum x1, waiting for transfers between devices, body(): lax.psum(for_sending(owned), 'rep')  26.4 us
    another operation x26, local copies, waits for them, and re-layouts  21.6 us
    unnamed x1, blocking collectives  17 us
    all_gather x1, blocking collectives, body(): lax.all_gather(output_projection_weight, 'group', axis=1, tiled=True)  14 us
  transfers between devices with their start and end apart: 15, of which 9 were waited for; matrix products, arithmetic and copies ran while one was open for 7% of the time, Pallas kernels for 0%

commit v1 on v0

--- a/solution.py
+++ b/solution.py
@@ -12,6 +12,12 @@
 MB = 2
 SLOTS = 1
 epsilon = 1e-06
+
+
+def derive_units(x_local, d0):
+    x_local = jnp.moveaxis(x_local, 0, d0)
+    v_next = x_local.shape
+    return x_local.reshape(*v_next[:d0], v_next[d0] * v_next[d0 + 1], *v_next[d0 + 2 :])
 
 
 def passed_along(value, axis, steps):
@@ -270,6 +276,21 @@
     first_dense_bias,
     second_dense_weight,
 ):
+
+    def build_slots(xin, mesh_ax, dimension_no):
+        parts_seen = []
+        t = 0
+        nodes = lax.psum(1, axis_name=mesh_ax)
+        while t < nodes:
+            parts_seen.append((t, (t + 1) % nodes))
+            t += 1
+        entries = [xin]
+        while len(entries) < nodes:
+            entries.append(lax.ppermute(entries[-1], axis_name=mesh_ax, perm=parts_seen))
+        plain = lax.axis_index(mesh_ax)
+        entries = jnp.stack(entries)[(plain - jnp.arange(nodes)) % nodes]
+        return derive_units(entries, dimension_no)
+
     is_first = lax.axis_index("section") == 0
     inputs_all = latents.reshape(MB, SLOTS, TOK, D)
     conds_all = cond.reshape(MB, SLOTS, D)
@@ -282,7 +303,7 @@
             lax.all_gather(adaptive_weight, "group", axis=1, tiled=True),
             lax.all_gather(adaptive_bias, "group", axis=1, tiled=True),
             lax.all_gather(query_key_value_weight, "group", axis=1, tiled=True),
-            lax.all_gather(output_projection_weight, "group", axis=1, tiled=True),
+            build_slots(output_projection_weight, "group", 1),
             lax.all_gather(first_dense_weight, "group", axis=1, tiled=True),
             lax.all_gather(first_dense_bias, "group", axis=1, tiled=True),
             lax.all_gather(second_dense_weight, "group", axis=1, tiled=True),

time: 584 us -> 584 us (level)
  blocking collectives: 97.2 us -> 82.2 us
  waiting for transfers between devices: 284 us -> 296 us
    ppermute x0 -> x3, waiting for transfers between devices: none -> 14.1 us  [build_slots(): lax.ppermute(entries[-1], axis_name=mesh_ax, perm=parts_seen)]
    all_gather x1 -> x0, blocking collectives: 14 us -> none  [body(): lax.all_gather(output_projection_weight, 'group', axis=1, tiled=True)]
  transfers between devices with their start and end apart: 15 -> 18, of which waited for: 9 -> 11; matrix products, arithmetic and copies ran while one was open for 7% -> 7% of each run, Pallas kernels for 0% -> 0%
where the time goes in v1:
time: 584 us; the launch traced here: 573 us
  waiting for transfers between devices  296 us (51%)
  blocking collectives  82.2 us (14%)
  matrix products  60.4 us (10%)
  other arithmetic  51.5 us (9%)
  local copies, waits for them, and re-layouts  51.4 us (9%)
  between operations  18.8 us (3%)
  starting transfers between devices  11.8 us (2%)
    reduce_scatter x5, waiting for transfers between devices, body(): lax.psum_scatter(for_sending(totals), 'group', scatter_dimension=0, tiled...  119 us
    ppermute x6, waiting for transfers between devices, passed_along(): lax.ppermute(value, axis, [(source, source + steps) for source in range(f...  95.1 us
    all_gather x1, waiting for transfers between devices, body(): lax.all_gather(adaptive_weight, 'group', axis=1, tiled=True)  39.3 us
    all_gather x1, blocking collectives, body(): lax.all_gather(query_key_value_weight, 'group', axis=1, tiled=True)  32.5 us
    psum x1, waiting for transfers between devices, body(): lax.psum(for_sending(owned), 'rep')  26.3 us
    another operation x26, local copies, waits for them, and re-layouts  21.6 us
    unnamed x1, blocking collectives  17 us
    ppermute x3, waiting for transfers between devices, build_slots(): lax.ppermute(entries[-1], axis_name=mesh_ax, perm=parts_seen)  14.1 us
  transfers between devices with their start and end apart: 18, of which 11 were waited for; matrix products, arithmetic and copies ran while one was open for 7% of the time, Pallas kernels for 0%

profile of v1, /device:TPU:0, one launch (start us, length us, event | category | flops | bytes accessed | tf_op | source)
XLA Modules:
  0.0 573.1 jit_solution(1915244248838444284)
XLA Ops:
  9.5 3.1 collective-permute-start
  13.2 1.9 convert_reduce_fusion.10
  16.5 32.5 %all_gather.20 = bf16[1,384,1152]{2,1,0:T(8,128)(2,1)S(1)} all-gather(bf16[1,96,1152]{2,1,0:T(8,128)(2,1)} %param.25), channel_id=1, replica_groups=mesh['section'=2,'group'=4,'rep'=4] {'group'}, dimensions={1}, use_global_device_ids=true | all-gather | bytes 1105920 | tf_op jit(solution)/shard_map/all_gather | solution.py:305
  50.4 11.9 %all_gather.22 = bf16[1,1536]{1,0:T(2,128)(2,1)S(1)} all-gather(bf16[1,384]{1,0:T(2,128)(2,1)S(1)} %copy-done.182), channel_id=1, replica_groups=mesh['section'=2,'group'=4,'rep'=4] {'group'}, dimensions={1}, use_global_device_ids=true | all-gather | bytes 3840 | tf_op jit(solution)/shard_map/all_gather | solution.py:308
  65.1 11.0 %all-reduce = bf16[2304]{0:T(1024)(128)(2,1)S(1)} all-reduce(bf16[2304]{0:T(1024)(128)(2,1)S(1)} %dynamic-update-slice), channel_id=1, replica_groups=mesh['section'=2,'group'=4,'rep'=4] {'group'}, use_global_device_ids=true, to_apply=%add | all-reduce | flops 2304 | bytes 9216 | tf_op jit(solution)/shard_map/squeeze | solution.py:263
  76.2 7.7 %collective-permute-done.1 = bf16[1,96,384]{2,1,0:T(8,128)(2,1)S(1)} collective-permute-done((bf16[1,96,384]{2,1,0:T(8,128)(2,1)S(1)}, bf16[1,96,384]{2,1,0:T(8,128)(2,1)S(1)}, u32[]{:S(2)}, u32[]{:S(2)}) %collective-permute-start.1) | collective-permute-done | bytes 73760 | tf_op jit(solution)/shard_map/ppermute | solution.py:289
  84.0 6.4 %collective-permute-done.2 = bf16[1,96,384]{2,1,0:T(8,128)(2,1)S(1)} collective-permute-done((bf16[1,96,384]{2,1,0:T(8,128)(2,1)S(1)}, bf16[1,96,384]{2,1,0:T(8,128)(2,1)S(1)}, u32[]{:S(2)}, u32[]{:S(2)}) %collective-permute-start.2) | collective-permute-done | bytes 73760 | tf_op jit(solution)/shard_map/ppermute | solution.py:289
  91.1 39.3 %all-gather.4.cloned.1.call-done = bf16[1,384,2304]{2,1,0:T(8,128)(2,1)} async-done(((bf16[1,96,2304]{2,1,0:T(8,128)(2,1)}), bf16[1,384,2304]{2,1,0:T(8,128)(2,1)}) %all-gather.4.cloned.1.call-update) | async-done | bytes 1769488 | tf_op jit(solution)/shard_map/all_gather | solution.py:303
  130.4 13.2 %conditional.4 = (bf16[1,256,384]{2,1,0:T(8,128)(2,1)S(1)}, f32[1,384]{1,0:T(1,128)}, f32[1,2304]{1,0:T(1,128)S(1)}, bf16[1,256,384]{2,1,0:T(8,128)(2,1)}, bf16[...) conditional(s32[]{:T(128)} %convert_element_type.491, () %tuple.65, ...), branch_computations={%region_0.1_spmd, %region_1.8_spmd} | conditional | flops 1021386368 | bytes 41346496 | solution.py:321
  130.4 1.8 convolution_reduce_fusion
  138.8 2.8 fusion.16
  141.6 1.9 fusion.29
  145.1 1.8 convolution_reduce_fusion.2
  156.9 10.2 %conditional.5 = (bf16[1,256,384]{2,1,0:T(8,128)(2,1)S(1)}, f32[1,384]{1,0:T(1,128)}, f32[1,2304]{1,0:T(1,128)}, bf16[1,256,384]{2,1,0:T(8,128)(2,1)}, bf16[1,25...) conditional(s32[]{:T(128)} %convert_element_type.509, () %tuple.67, ...), branch_computations={%region_14.15_spmd, %region_15.22_spmd} | conditional | flops 1021386368 | bytes 41874824 | solution.py:321
  167.1 9.5 %conditional.6 = (f32[384,2304]{1,0:T(8,128)}, f32[2304]{0:T(1024)S(1)}, f32[1536]{0:T(1024)S(1)}, bf16[1,256,384]{2,1,0:T(8,128)(2,1)S(1)}, bf16[1,384]{1,0:T(2...) conditional(s32[]{:T(128)} %convert_element_type.509, () %tuple.70, ...), branch_computations={%region_22.23_spmd, %region_23.40_spmd} | conditional | flops 2089162752 | bytes 87958680 | solution.py:344
  174.6 2.0 broadcast.961
  178.1 92.8 %collective-permute-done.5 = bf16[1,256,384]{2,1,0:T(8,128)(2,1)S(1)} collective-permute-done((bf16[1,256,384]{2,1,0:T(8,128)(2,1)S(1)}, bf16[1,256,384]{2,1,0:T(8,128)(2,1)S(1)}, u32[]{:S(2)}, u32[]{:S(2)}) %collective-permute-start.5) | collective-permute-done | bytes 196640 | tf_op jit(solution)/shard_map/ppermute | solution.py:26
  271.0 4.6 convert_reduce_fusion.8
  277.6 2.1 fusion.169
  290.9 2.0 collective-permute-done.6
  293.8 58.3 %conditional.7 = (f32[1,256,384]{2,1,0:T(8,128)}, f32[1,384]{1,0:T(1,128)}, f32[384,2304]{1,0:T(8,128)}, f32[2304]{0:T(1024)}, f32[1536]{0:T(1024)}, /*index=5*/...) conditional(s32[]{:T(128)} %convert_element_type.491, () %tuple.69, ...), branch_computations={%region_45.46_spmd, %region_46.63_spmd} | conditional | flops 2088473856 | bytes 92844544 | solution.py:344
  297.5 2.0 convert_reduce_fusion.7
  299.4 1.8 multiply_reduce_fusion.7
  301.3 3.6 convert_reduce_fusion.5
  310.5 1.9 multiply_reduce_fusion.8
  316.5 2.1 convolution_bitcast_fusion.9
  318.6 2.1 copy.164
  320.7 2.1 copy.131
  331.4 2.0 add_add_fusion.5
  335.7 1.9 copy.162
  337.6 3.3 convolution_bitcast_fusion.5
  340.9 3.2 copy.168
  344.1 2.0 convolution_bitcast_fusion.6
  346.1 3.2 copy.166
  349.3 2.9 broadcast_multiply_fusion.7
  352.1 2.3 add_convert_fusion.7
  354.6 3.7 add_convert_fusion.6
  358.7 4.1 add_convert_fusion.5
  362.9 5.7 add_convert_fusion.4
  371.0 4.9 add_convert_fusion.3
  380.3 18.7 %reduce-scatter.8.cloned.1.call-done = bf16[96,1152]{1,0:T(8,128)(2,1)} async-done(((bf16[384,1152]{1,0:T(8,128)(2,1)}), bf16[96,1152]{1,0:T(8,128)(2,1)}) %reduce-scatter.8.cloned.1.call-update) | async-done | bytes 221200 | tf_op jit(solution)/shard_map/reduce_scatter | solution.py:359
  399.0 30.4 %reduce-scatter.12.cloned.1.call-done = bf16[96,1536]{1,0:T(8,128)(2,1)} async-done(((bf16[384,1536]{1,0:T(8,128)(2,1)}), bf16[96,1536]{1,0:T(8,128)(2,1)}) %reduce-scatter.12.cloned.1.call-update) | async-done | bytes 294928 | tf_op jit(solution)/shard_map/reduce_scatter | solution.py:359
  429.5 30.2 %reduce-scatter.14.cloned.1.call-done = bf16[384,384]{1,0:T(8,128)(2,1)} async-done(((bf16[1536,384]{1,0:T(8,128)(2,1)}), bf16[384,384]{1,0:T(8,128)(2,1)}) %reduce-scatter.14.cloned.1.call-update) | async-done | bytes 294928 | tf_op jit(solution)/shard_map/reduce_scatter | solution.py:359
  459.7 39.5 %reduce-scatter.6.cloned.1.call-done = bf16[96,2304]{1,0:T(8,128)(2,1)} async-done(((bf16[384,2304]{1,0:T(8,128)(2,1)}), bf16[96,2304]{1,0:T(8,128)(2,1)}) %reduce-scatter.6.cloned.1.call-update) | async-done | bytes 442384 | tf_op jit(solution)/shard_map/reduce_scatter | solution.py:359
  502.5 17.0 %all-reduce.5 = (bf16[2304]{0:T(1024)(128)(2,1)S(1)}, bf16[1536]{0:T(1024)(128)(2,1)S(1)}) all-reduce(bf16[2304]{0:T(1024)(128)(2,1)S(1)} %add_convert_fusion.9, bf16[1536]{0:T(1024)(128)(2,1)S(1)} %add_convert_fusion.10), channel_id=3, replica_groups=mesh['section'=2,'group'=4,'rep'=4] {'group'}, use_global_device_ids=true, to_apply=%region_71.72.clone | all-reduce | flops 3840 | bytes 15360
  519.7 9.8 %all-reduce.3 = (bf16[1,576]{1,0:T(2,128)(2,1)S(1)}, bf16[1,384]{1,0:T(2,128)(2,1)S(1)}) all-reduce(bf16[1,576]{1,0:T(2,128)(2,1)S(1)} %broadcast_in_dim.142, bf16[1,384]{1,0:T(2,128)(2,1)S(1)} %broadcast_in_dim.150), channel_id=1, replica_groups=mesh['section'=2,'group'=4,'rep'=4] {'rep'}, use_global_device_ids=true, to_apply=%region_72.73 | all-reduce | flops 960 | bytes 3840 | tf_op jit(solution)/shard_map/psum | solution.py:361
  533.9 26.3 %all-reduce.8.cloned.1.call-done = (bf16[1,96,2304]{2,1,0:T(8,128)(2,1)}, bf16[1,96,1152]{2,1,0:T(8,128)(2,1)}, bf16[1,96,384]{2,1,0:T(8,128)(2,1)}, bf16[1,96,1536]{2,1,0:T(8,128)(2,1)}, bf16[1,384,384]{2,1,0:T(8,128)(2,1)}) async-done(((bf16[1,96,2304]{2,1,0:T(8,128)(2,1)}, bf16[1,96,1152]{2,1,0:T(8,128)(2,1)}, bf16[1,96,384]{2,1,0:T(8,128)(2,1)}, bf16[1,96,1536]{2,1,0:T(8,128)(2,1)}, ...) | async-done | bytes 1327120 | tf_op jit(solution)/shard_map/psum | solution.py:361
  561.9 2.0 broadcast_in_dim.141
  (508 shorter events, 98.6 us)
Async XLA Ops:
  7.2 56.4 %copy-start.179 = (u32[32]{0:T(128)S(1)}, u32[32]{0:T(128)}, u32[]{:S(2)}) copy-start(u32[32]{0:T(128)} %constant.323) | copy-start | bytes 388
  7.2 83.2 %copy-start.111 = (bf16[1,96,384]{2,1,0:T(8,128)(2,1)S(1)}, bf16[1,96,384]{2,1,0:T(8,128)(2,1)}, u32[]{:S(2)}) copy-start(bf16[1,96,384]{2,1,0:T(8,128)(2,1)} %param.26) | copy-start | bytes 221188
  7.2 43.1 %copy-start.178 = (bf16[1,576]{1,0:T(2,128)(2,1)S(1)}, bf16[1,576]{1,0:T(2,128)(2,1)}, u32[]{:S(2)}) copy-start(bf16[1,576]{1,0:T(2,128)(2,1)} %param.24) | copy-start | bytes 3460
  7.2 43.1 %copy-start.182 = (bf16[1,384]{1,0:T(2,128)(2,1)S(1)}, bf16[1,384]{1,0:T(2,128)(2,1)}, u32[]{:S(2)}) copy-start(bf16[1,384]{1,0:T(2,128)(2,1)} %param.28) | copy-start | bytes 2308
  7.2 55.6 %copy-start.64 = (bf16[2,256,384]{2,1,0:T(8,128)(2,1)S(1)}, bf16[2,256,384]{2,1,0:T(8,128)(2,1)}, u32[]{:S(2)}) copy-start(bf16[2,256,384]{2,1,0:T(8,128)(2,1)} %param.19) | copy-start | bytes 1179652
  7.2 83.8 %all-gather.6.cloned.1.call-start = ((), (), s32[]{:S(2)}) async-start(), calls=%async_computation.6 | async-start | bytes 1474560 | tf_op jit(solution)/shard_map/all_gather | solution.py:307
  8.0 83.1 %all-gather.8.cloned.1.call-start = ((), (), s32[]{:S(2)}) async-start(), calls=%async_computation.7 | async-start | bytes 1474560 | tf_op jit(solution)/shard_map/all_gather | solution.py:309
  8.7 121.7 %all-gather.4.cloned.1.call-start = ((), (), s32[]{:S(2)}) async-start(), calls=%async_computation.5 | async-start | bytes 2211840 | tf_op jit(solution)/shard_map/all_gather | solution.py:303
  9.5 370.8 %reduce-scatter.10.cloned.1.call-start = ((), (), s32[]{:S(2)}) async-start(), calls=%async_computation.10 | async-start | bytes 368640 | tf_op jit(solution)/shard_map/reduce_scatter | solution.py:359
  9.5 66.7 %collective-permute-start = (bf16[1,96,384]{2,1,0:T(8,128)(2,1)}, bf16[1,96,384]{2,1,0:T(8,128)(2,1)S(1)}, u32[]{:S(2)}, u32[]{:S(2)}) collective-permute-start(bf16[1,96,384]{2,1,0:T(8,128)(2,1)} %param.26), channel_id=1, source_target_pairs={{0,4},{4,8},{8,12},{12,0},{1,5},{5,9},{9,13},{13,1},{2,6},{6,10},{... | collective-permute-start | bytes 221192 | tf_op jit(solution)/shard_map/ppermute | solution.py:289
  49.0 99.0 %copy-start.6 = (bf16[1,384,1152]{2,1,0:T(8,128)(2,1)}, bf16[1,384,1152]{2,1,0:T(8,128)(2,1)S(1)}, u32[]{:S(2)}) copy-start(bf16[1,384,1152]{2,1,0:T(8,128)(2,1)S(1)} %all_gather.20) | copy-start | bytes 2654212
  62.3 68.2 %copy-start.112 = (bf16[1536]{0:T(1024)(128)(2,1)}, bf16[1536]{0:T(1024)(128)(2,1)S(1)}, u32[]{:S(2)}) copy-start(bf16[1536]{0:T(1024)(128)(2,1)S(1)} %reduce.132) | copy-start | bytes 9220
  76.2 7.8 %collective-permute-start.1 = (bf16[1,96,384]{2,1,0:T(8,128)(2,1)S(1)}, bf16[1,96,384]{2,1,0:T(8,128)(2,1)S(1)}, u32[]{:S(2)}, u32[]{:S(2)}) collective-permute-start(bf16[1,96,384]{2,1,0:T(8,128)(2,1)S(1)} %collective-permute-done), channel_id=1, source_target_pairs={{0,4},{4,8},{8,12},{12,0},{1,5},{5,9},{9,13},{13,1},{2,6},{6,10},{... | collective-permute-start | bytes 221192 | tf_op jit(solution)/shard_map/ppermute | solution.py:289
  84.0 6.4 %collective-permute-start.2 = (bf16[1,96,384]{2,1,0:T(8,128)(2,1)S(1)}, bf16[1,96,384]{2,1,0:T(8,128)(2,1)S(1)}, u32[]{:S(2)}, u32[]{:S(2)}) collective-permute-start(bf16[1,96,384]{2,1,0:T(8,128)(2,1)S(1)} %collective-permute-done.1), channel_id=1, source_target_pairs={{0,4},{4,8},{8,12},{12,0},{1,5},{5,9},{9,13},{13,1},{2,6},{6,10},{... | collective-permute-start | bytes 221192 | tf_op jit(solution)/shard_map/ppermute | solution.py:289
  91.0 59.3 %copy-start.1 = (bf16[4,96,384]{2,1,0:T(8,128)(2,1)}, bf16[4,96,384]{2,1,0:T(8,128)(2,1)S(1)}, u32[]{:S(2)}) copy-start(bf16[4,96,384]{2,1,0:T(8,128)(2,1)S(1)} %gather_fusion) | copy-start | bytes 884740
  143.6 5.0 copy-start.25
  143.6 5.0 copy-start.36
  143.6 4.0 collective-permute-start.3
  154.5 2.3 collective-permute-start.4
  176.6 94.3 %copy-start.107 = (f32[2304]{0:T(1024)}, f32[2304]{0:T(1024)S(1)}, u32[]{:S(2)}) copy-start(f32[2304]{0:T(1024)S(1)} %get-tuple-element.381) | copy-start | bytes 27652
  176.6 94.3 %copy-start.124 = (f32[1536]{0:T(1024)}, f32[1536]{0:T(1024)S(1)}, u32[]{:S(2)}) copy-start(f32[1536]{0:T(1024)S(1)} %get-tuple-element.389) | copy-start | bytes 18436
  176.6 94.3 %collective-permute-start.5 = (bf16[1,256,384]{2,1,0:T(8,128)(2,1)S(1)}, bf16[1,256,384]{2,1,0:T(8,128)(2,1)S(1)}, u32[]{:S(2)}, u32[]{:S(2)}) collective-permute-start(bf16[1,256,384]{2,1,0:T(8,128)(2,1)S(1)} %get-tuple-element.363), channel_id=1, source_target_pairs={{16,0},{17,1},{18,2},{19,3},{20,4},{21,5},{22,6},{23,7},{24,8},{25... | collective-permute-start | bytes 589832 | tf_op jit(solution)/shard_map/ppermute | solution.py:26
  270.9 6.7 %copy-start.91 = (bf16[1,256,384]{2,1,0:T(8,128)(2,1)}, bf16[1,256,384]{2,1,0:T(8,128)(2,1)S(1)}, u32[]{:S(2)}) copy-start(bf16[1,256,384]{2,1,0:T(8,128)(2,1)S(1)} %collective-permute-done.5) | copy-start | bytes 589828
  288.4 5.4 copy-start.60
  288.4 5.4 copy-start.3
  288.4 5.4 copy-start.11
  288.4 5.3 copy-start.26
  288.5 5.3 copy-start.110
  289.6 3.3 collective-permute-start.6
  299.4 5.4 copy-start.162
  327.6 5.8 %copy-start.134 = (f32[1,384]{1,0:T(1,128)S(1)}, f32[1,384]{1,0:T(1,128)}, u32[]{:S(2)}) copy-start(f32[1,384]{1,0:T(1,128)} %get-tuple-element.282) | copy-start | bytes 4612 | tf_op jit(solution)/shard_map/cond
  327.6 5.8 %copy-start.168 = (f32[1,384]{1,0:T(1,128)S(1)}, f32[1,384]{1,0:T(1,128)}, u32[]{:S(2)}) copy-start(f32[1,384]{1,0:T(1,128)} %get-tuple-element.680) | copy-start | bytes 4612 | tf_op jit(solution)/shard_map/cond
  354.5 44.5 %reduce-scatter.8.cloned.1.call-start = ((), (), s32[]{:S(2)}) async-start(), calls=%async_computation.9 | async-start | bytes 1105920 | tf_op jit(solution)/shard_map/reduce_scatter | solution.py:359
  358.4 71.1 %reduce-scatter.12.cloned.1.call-start = ((), (), s32[]{:S(2)}) async-start(), calls=%async_computation.11 | async-start | bytes 1474560 | tf_op jit(solution)/shard_map/reduce_scatter | solution.py:359
  362.8 96.9 %reduce-scatter.14.cloned.1.call-start = ((), (), s32[]{:S(2)}) async-start(), calls=%async_computation.12 | async-start | bytes 1474560 | tf_op jit(solution)/shard_map/reduce_scatter | solution.py:359
  362.9 5.8 %copy-start.177 = (bf16[384]{0:T(512)(128)(2,1)S(1)}, bf16[384]{0:T(512)(128)(2,1)}, u32[]{:S(2)}) copy-start(bf16[384]{0:T(512)(128)(2,1)} %get-tuple-element.687) | copy-start | bytes 2308
  362.9 5.8 %copy-start.59 = (f32[256,384]{1,0:T(8,128)S(1)}, f32[256,384]{1,0:T(8,128)}, u32[]{:S(2)}) copy-start(f32[256,384]{1,0:T(8,128)} %copy-done.58) | copy-start | bytes 1179652
  368.6 130.5 %reduce-scatter.6.cloned.1.call-start = ((), (), s32[]{:S(2)}) async-start(), calls=%async_computation.8 | async-start | bytes 2211840 | tf_op jit(solution)/shard_map/reduce_scatter | solution.py:359
  375.9 123.3 %copy-start.146 = (f32[1,384]{1,0:T(1,128)S(1)}, f32[1,384]{1,0:T(1,128)}, u32[]{:S(2)}) copy-start(f32[1,384]{1,0:T(1,128)} %get-tuple-element.688) | copy-start | bytes 4612
  375.9 184.4 %all-reduce.8.cloned.1.call-start = ((), (), s32[]{:S(2)}) async-start(), calls=%async_computation.13 | async-start | bytes 2654208 | tf_op jit(solution)/shard_map/psum | solution.py:361
  378.1 152.6 %collective-permute-start.8 = (bf16[1,384]{1,0:T(2,128)(2,1)S(1)}, bf16[1,384]{1,0:T(2,128)(2,1)S(1)}, u32[]{:S(2)}, u32[]{:S(2)}) collective-permute-start(bf16[1,384]{1,0:T(2,128)(2,1)S(1)} %copy-done.181), channel_id=1, source_target_pairs={{16,0},{17,1},{18,2},{19,3},{20,4},{21,5},{22,6},{23,7},{24,8},{25... | collective-permute-start | bytes 2312 | tf_op jit(solution)/shard_map/ppermute | solution.py:26
  380.3 120.8 %copy-start.125 = (f32[1536]{0:T(1024)S(1)}, f32[1536]{0:T(1024)}, u32[]{:S(2)}) copy-start(f32[1536]{0:T(1024)} %copy-done.124) | copy-start | bytes 18436
  380.3 120.8 %copy-start.167 = (f32[1536]{0:T(1024)S(1)}, f32[1536]{0:T(1024)}, u32[]{:S(2)}) copy-start(f32[1536]{0:T(1024)} %get-tuple-element.772) | copy-start | bytes 18436
  499.1 31.5 %copy-start.169 = (f32[1,384]{1,0:T(1,128)S(1)}, f32[1,384]{1,0:T(1,128)}, u32[]{:S(2)}) copy-start(f32[1,384]{1,0:T(1,128)} %get-tuple-element.378) | copy-start | bytes 4612
  499.2 32.8 %copy-start.76 = (bf16[1,256,384]{2,1,0:T(8,128)(2,1)S(1)}, bf16[1,256,384]{2,1,0:T(8,128)(2,1)}, u32[]{:S(2)}) copy-start(bf16[1,256,384]{2,1,0:T(8,128)(2,1)} %copy-done.75) | copy-start | bytes 589828
  499.2 33.8 %copy-start.55 = (f32[1,256,384]{2,1,0:T(8,128)S(1)}, f32[1,256,384]{2,1,0:T(8,128)}, u32[]{:S(2)}) copy-start(f32[1,256,384]{2,1,0:T(8,128)} %get-tuple-element.748) | copy-start | bytes 1179652
  499.8 30.9 %collective-permute-start.7 = (bf16[1,384]{1,0:T(2,128)(2,1)S(1)}, bf16[1,384]{1,0:T(2,128)(2,1)S(1)}, u32[]{:S(2)}, u32[]{:S(2)}) collective-permute-start(bf16[1,384]{1,0:T(2,128)(2,1)S(1)} %get-tuple-element.770), channel_id=1, source_target_pairs={{16,0},{17,1},{18,2},{19,3},{20,4},{21,5},{22,6},{23,7},{24,8},{25... | collective-permute-start | bytes 2312 | tf_op jit(solution)/shard_map/ppermute | solution.py:26
  560.3 5.3 copy-start.99
  (123 other events, 296.4 us)
Sparse Core Ops, SparseCore 0:
  9.6 44.5 all-gather.5
  55.8 33.1 all-gather.7
  90.6 39.7 all-gather.3
  354.6 18.7 reduce-scatter.9
  376.2 22.8 reduce-scatter.7
  401.2 28.2 reduce-scatter.11
  431.8 27.8 reduce-scatter.13
  462.0 37.0 reduce-scatter.5
  503.2 57.0 all-reduce.7
